TPU v7x, 512 devices: a whole 4x4x16 slice. The times are simulated.
512 devices in a mesh: lev: 4 (over y), tile: 64 (over z_lo, x, core), sec: 2 (over z_hi).
Axes of the slice: x: 4, y: 4, z: 16 (z_hi: 2, z_lo: 8; z = z_hi * 8 + z_lo), core: 2. Of those that a mesh axis runs over, the one named last changes fastest.
Arguments:
- fields: float32 [3, 64, 4, 128, 360], P(None, ('lev', 'sec'), None, 'tile'), may hold values from -6 to 6
- surface: float32 [4, 128, 360], P(None, 'tile'), may hold values from -6 to 6
- cot_fields: float32 [3, 64, 4, 128, 360], P(None, ('lev', 'sec'), None, 'tile'), may hold values from -6 to 6
- cot_surface: float32 [4, 128, 360], P(None, 'tile'), may hold values from -6 to 6
- land_sea: int32 [128, 360], P('tile'), may hold values 0 or 1
- w_in: bfloat16 [192, 384], replicated, may hold values from -0.4375 to 0.4375
- w_mid: bfloat16 [384, 384], replicated, may hold values from -0.3125 to 0.3125
- w_out: bfloat16 [384, 192], replicated, may hold values from -0.3125 to 0.3125
- bias_in: float32 [2, 384], replicated, may hold values from -4 to 4
Outputs:
- final_fields: float32 [3, 64, 4, 128, 360], P(None, ('lev', 'sec'), None, 'tile')
- final_surface: float32 [4, 128, 360], P(None, 'tile')
- fields_grad: float32 [3, 64, 4, 128, 360], P(None, ('lev', 'sec'), None, 'tile')
- surface_grad: float32 [4, 128, 360], P(None, 'tile')
- w_in_grad: float32 [192, 384], replicated
- w_mid_grad: float32 [384, 384], replicated
- w_out_grad: float32 [384, 192], replicated
- bias_grad: float32 [2, 384], replicated
Inputs may be any that keep to these rules, and one draw needn't show every extreme that they name: `land_sea`: 1 marks land, 0 sea.
All inputs are finite; a program needn't handle non-finite values. No bound on the sum of `land_sea` on one device may be relied on, other than what follows from the above.
Results may differ from a plain program's by a relative error of at most 0.005.
Values may be sent and summed in bfloat16 or wider, within the bound.
A program may use at most 64 MiB of HBM per device.

v0:
```python
import math
import jax
import jax.numpy as jnp
from jax import lax
from jax.sharding import PartitionSpec as P

NLEV = 64
STEPS = 2
TIME_STEP = 0.1
COS_FLOOR = 0.2
INV_SQRT_TWO = 1.0 / math.sqrt(2.0)
INV_SQRT_TWO_PI = 1.0 / math.sqrt(2.0 * math.pi)


def extended(value, sides, width):
    for axis, dim in sides:
        size, length = (lax.axis_size(axis), value.shape[dim])
        up = [(i, (i + 1) % size) for i in range(size - 1)]
        down = [(j, i) for i, j in up]
        last = lax.slice_in_dim(value, length - width, length, axis=dim)
        first = lax.slice_in_dim(value, 0, width, axis=dim)
        before = lax.ppermute(last, axis, up)
        after = lax.ppermute(first, axis, down)
        value = jnp.concatenate([before, value, after], axis=dim)
    return value


def carried_in(part, axis, combine, identity):
    place = lax.axis_index(axis)
    gathered = jax.tree.map(lambda a: lax.all_gather(a, axis), part)
    state = jax.tree.map(lambda a, e: jnp.zeros_like(a) + jnp.asarray(e, a.dtype), part, identity)

    def one(lap, state):
        return combine(
            state, jax.tree.map(lambda a: lax.dynamic_index_in_dim(a, lap, 0, False), gathered)
        )

    return lax.fori_loop(0, place, one, state)


def gelu_slope(values):
    cumulative = 0.5 * (1.0 + lax.erf(values * INV_SQRT_TWO))
    density = jnp.exp(-0.5 * values * values) * INV_SQRT_TWO_PI
    return cumulative + values * density


def lon_change(values, x_factor):
    return (jnp.roll(values, -1, axis=-1) - jnp.roll(values, 1, axis=-1)) * x_factor


def lat_change(values):
    padded = extended(values, (("tile", 2),), 1)
    return (padded[:, :, 2:, :] - padded[:, :, :-2, :]) * 0.5


def add_pairs(earlier, later):
    return (earlier[0] + later[0], earlier[1] + later[1])


def vertical_sums(rising_in, falling_in):
    rising_run = jnp.cumsum(rising_in, axis=0)
    falling_run = jnp.flip(jnp.cumsum(jnp.flip(falling_in, 0), axis=0), 0)
    rising_part = rising_run[-1]
    falling_part = falling_run[0]
    zeros_part = jnp.zeros_like(rising_part)
    before, falling_before = carried_in(
        (rising_part, falling_part), ("lev", "sec"), add_pairs, (zeros_part, zeros_part)
    )
    column_sum, falling_total = lax.psum((rising_part, falling_part), ("lev", "sec"))
    beyond = falling_total - falling_before - falling_part
    return (before + rising_run, beyond + falling_run, column_sum)


def on_device(fields, surface, cot_fields, cot_surface, land_sea, w_in, w_mid, w_out, bias_in):
    lev_dev = fields.shape[1]
    batch_size = fields.shape[2]
    lat_dev = fields.shape[3]
    lon_cells = fields.shape[4]
    level_shape = fields.shape
    shard_count = lax.axis_size(("lev", "sec"))
    position = lax.axis_index(("lev", "sec"))
    lat_total = lat_dev * lax.axis_size("tile")
    row_ids = (lax.axis_index("tile") * lat_dev + jnp.arange(lat_dev)).astype(jnp.float32)
    latitude = -0.5 * math.pi + (row_ids + 0.5) * (math.pi / lat_total)
    x_factor = (0.5 / jnp.maximum(jnp.cos(latitude), COS_FLOOR))[:, None]
    sin_lat = jnp.sin(latitude)[:, None]
    level_ids = (position * lev_dev + jnp.arange(lev_dev)).astype(jnp.float32)
    layer_thickness_fraction = (1.0 / (level_ids + 1.0))[:, None, None, None]
    col_count = batch_size * lat_dev * lon_cells // shard_count
    mask_all = jnp.broadcast_to(land_sea[None], (batch_size, lat_dev, lon_cells)).reshape(-1)
    mask_cols = lax.dynamic_slice_in_dim(mask_all, position * col_count, col_count)
    land_cols = (mask_cols > 0)[None, :]
    bias_cols = jnp.where(mask_cols[None, :] > 0, bias_in[1][:, None], bias_in[0][:, None])

    def to_columns(values):
        flattened = values.reshape(values.shape[0], values.shape[1], -1)
        arrived = lax.all_to_all(flattened, ("lev", "sec"), split_axis=2, concat_axis=1, tiled=True)
        return arrived.reshape(arrived.shape[0] * arrived.shape[1], arrived.shape[2])

    def to_levels(values):
        regrouped = values.reshape(level_shape[0], -1, values.shape[1])
        arrived = lax.all_to_all(regrouped, ("lev", "sec"), split_axis=1, concat_axis=2, tiled=True)
        return arrived.reshape(level_shape)

    current_fields_bundle, current_ground_pressure = (fields, surface)
    stored = []
    for instant in range(STEPS):
        x_cols = to_columns(current_fields_bundle.astype(jnp.bfloat16))
        first_pre = (
            jnp.einsum("fh,fc->hc", w_in, x_cols, preferred_element_type=jnp.float32) + bias_cols
        )
        first_act = jax.nn.gelu(first_pre, approximate=False).astype(jnp.bfloat16)
        second_pre = jnp.einsum("io,ic->oc", w_mid, first_act, preferred_element_type=jnp.float32)
        second_act = jax.nn.gelu(second_pre, approximate=False).astype(jnp.bfloat16)
        first_pre, first_act, second_pre, second_act = (
            first_pre,
            first_act,
            second_pre,
            second_act,
        )
        tendency = jnp.einsum(
            "hf,hc->fc", w_out, second_act, preferred_element_type=jnp.float32
        ).astype(jnp.bfloat16)
        zonal_velocity = current_fields_bundle[0]
        meridional_velocity = current_fields_bundle[1]
        thermal_field = current_fields_bundle[2]
        velocity_spreading = lon_change(zonal_velocity, x_factor) + lat_change(meridional_velocity)
        dynamics_prefix, dynamics_suffix, dynamics_column_sum = vertical_sums(
            velocity_spreading, layer_thickness_fraction * thermal_field
        )
        gravity_potential_elevation = dynamics_suffix + current_ground_pressure[None]
        zonal_tend = (
            -lon_change(gravity_potential_elevation, x_factor) + sin_lat * meridional_velocity
        )
        merid_tend = -lat_change(gravity_potential_elevation) - sin_lat * zonal_velocity
        temp_tend = -(dynamics_prefix / NLEV)
        dyn_fields = jnp.stack([zonal_tend, merid_tend, temp_tend])
        dyn_surface = -dynamics_column_sum / NLEV
        physics = to_levels(tendency).astype(jnp.float32)
        current_fields_bundle = current_fields_bundle + TIME_STEP * (dyn_fields + physics)
        current_ground_pressure = current_ground_pressure + TIME_STEP * dyn_surface
        stored.append((x_cols, first_pre, first_act, second_pre, second_act))
    field_bar, surface_bar = (cot_fields, cot_surface)
    gradient = (
        jnp.zeros(w_in.shape, jnp.float32),
        jnp.zeros(w_mid.shape, jnp.float32),
        jnp.zeros(w_out.shape, jnp.float32),
        jnp.zeros(bias_in.shape, jnp.float32),
    )
    for instant in reversed(range(STEPS)):
        x_cols, first_pre, first_act, second_pre, second_act = stored[instant]
        tend_bar = to_columns((TIME_STEP * field_bar).astype(jnp.bfloat16))
        second_bar = (
            jnp.einsum("hf,fc->hc", w_out, tend_bar, preferred_element_type=jnp.float32)
            * gelu_slope(second_pre)
        ).astype(jnp.bfloat16)
        first_bar = (
            jnp.einsum("io,oc->ic", w_mid, second_bar, preferred_element_type=jnp.float32)
            * gelu_slope(first_pre)
        ).astype(jnp.bfloat16)
        input_bar = jnp.einsum(
            "fh,hc->fc", w_in, first_bar, preferred_element_type=jnp.float32
        ).astype(jnp.bfloat16)
        first_wide = first_bar.astype(jnp.float32)
        zero_f = jnp.zeros((), jnp.float32)
        sea_part = jnp.sum(jnp.where(land_cols, zero_f, first_wide), axis=1)
        land_part = jnp.sum(jnp.where(land_cols, first_wide, zero_f), axis=1)
        local_grads = (
            jnp.einsum("fc,hc->fh", x_cols, first_bar, preferred_element_type=jnp.float32),
            jnp.einsum("ic,oc->io", first_act, second_bar, preferred_element_type=jnp.float32),
            jnp.einsum("hc,fc->hf", second_act, tend_bar, preferred_element_type=jnp.float32),
            jnp.stack([sea_part, land_part]),
        )
        a_zonal = field_bar[0]
        a_merid = field_bar[1]
        a_temp = field_bar[2]
        height_bar = lon_change(a_zonal, x_factor) + lat_change(a_merid)
        prefix, suffix, column_sum = vertical_sums(height_bar, a_temp)
        temp_bar = layer_thickness_fraction * prefix
        div_bar = (-suffix - surface_bar[None]) / NLEV
        zonal_bar = -lon_change(div_bar, x_factor) - sin_lat * a_merid
        merid_bar = -lat_change(div_bar) + sin_lat * a_zonal
        adj_fields = jnp.stack([zonal_bar, merid_bar, temp_bar])
        input_levels = to_levels(input_bar).astype(jnp.float32)
        field_bar = field_bar + TIME_STEP * adj_fields + input_levels
        surface_bar = surface_bar + TIME_STEP * column_sum
        summed = lax.psum(
            (local_grads[0], local_grads[1], local_grads[2], local_grads[3]), ("lev", "tile", "sec")
        )
        gradient = jax.tree.map(jnp.add, gradient, summed)
    return (
        current_fields_bundle,
        current_ground_pressure,
        field_bar,
        surface_bar,
        gradient[0],
        gradient[1],
        gradient[2],
        gradient[3],
    )


def solution(mesh):
    return jax.shard_map(
        on_device,
        mesh=mesh,
        in_specs=(
            P(None, ("lev", "sec"), None, "tile", None),
            P(None, "tile", None),
            P(None, ("lev", "sec"), None, "tile", None),
            P(None, "tile", None),
            P("tile", None),
            P(),
            P(),
            P(),
            P(),
        ),
        out_specs=(
            P(None, ("lev", "sec"), None, "tile", None),
            P(None, "tile", None),
            P(None, ("lev", "sec"), None, "tile", None),
            P(None, "tile", None),
            P(),
            P(),
            P(),
            P(),
        ),
        check_vma=False,
    )
```

profile of v0, /device:TPU:8, one launch (start us, length us, event | category | flops | bytes accessed | tf_op | source)
XLA Modules:
  0.0 1526.2 jit_solution(4728833632779786206)
XLA Ops:
  11.7 3.6 collective-permute-start.1
  19.7 3.7 collective-permute-start.9
  25.1 4.8 copy.305
  30.0 2.8 reshape.435
  32.7 18.2 %all-to-all-start = ((bf16[8,2,4320]{2,1,0:T(2,128)(2,1)}), bf16[8,2,4320]{2,1,0:T(2,128)(2,1)}, u32[]{:S(2)}, u32[]{:S(2)}) async-start(bf16[8,2,4320]{2,1,0:T(2,128)(2,1)} %reshape.435), calls=%async_computation | async-start | bytes 278528 | tf_op jit(solution)/shard_map/all_to_all | solution.py:97
  62.3 63.0 %all_gather.29 = f32[8,4,2,360]{3,1,2,0:T(4,128)} all-gather(f32[1,4,2,360]{3,1,2,0:T(4,128)S(1)} %copy.336), channel_id=1, replica_groups=mesh['lev'=4,'tile'=64,'sec'=2] {'lev','sec'}, dimensions={0}, use_global_device_ids=true | all-gather | bytes 103680 | tf_op jit(solution)/shard_map/all_gather | solution.py:30
  125.9 78.4 %all-reduce.2 = (f32[4,2,360]{2,1,0:T(2,128)}, f32[4,2,360]{2,1,0:T(2,128)}) all-reduce(f32[4,2,360]{2,1,0:T(2,128)S(1)} %get-tuple-element.428, f32[4,2,360]{2,1,0:T(2,128)S(1)} %get-tuple-element.453), channel_id=1, replica_groups=mesh['lev'=4,'tile'=64,'sec'=2] {'lev','sec'}, use_global_device_ids=true, to_apply=%region_1.2 | all-reduce | flops 5760 | bytes 46080 | tf_op jit(solution)/shard_map/psum | solution.py:69
  204.3 2.7 copy.380
  207.0 2.8 reshape.439
  209.8 63.3 %all_gather.25 = f32[8,4,2,360]{3,1,2,0:T(4,128)S(1)} all-gather(f32[1,4,2,360]{3,1,2,0:T(4,128)S(1)} %copy.295), channel_id=1, replica_groups=mesh['lev'=4,'tile'=64,'sec'=2] {'lev','sec'}, dimensions={0}, use_global_device_ids=true | all-gather | bytes 103680 | tf_op jit(solution)/shard_map/all_gather | solution.py:30
  275.2 63.2 %all_gather.24 = f32[8,4,2,360]{3,1,2,0:T(4,128)S(1)} all-gather(f32[1,4,2,360]{3,1,2,0:T(4,128)S(1)} %copy.294), channel_id=1, replica_groups=mesh['lev'=4,'tile'=64,'sec'=2] {'lev','sec'}, dimensions={0}, use_global_device_ids=true | all-gather | bytes 103680 | tf_op jit(solution)/shard_map/all_gather | solution.py:30
  343.8 62.9 %all_gather.28 = f32[8,4,2,360]{3,1,2,0:T(4,128)S(1)} all-gather(f32[1,4,2,360]{3,1,2,0:T(4,128)S(1)} %copy.335), channel_id=1, replica_groups=mesh['lev'=4,'tile'=64,'sec'=2] {'lev','sec'}, dimensions={0}, use_global_device_ids=true | all-gather | bytes 103680 | tf_op jit(solution)/shard_map/all_gather | solution.py:30
  411.7 3.6 collective-permute-start.3
  417.2 3.6 collective-permute-start.11
  422.9 8.4 all-to-all-start.4
  431.4 3.0 reshape.436
  434.4 2.2 copy.376
  436.6 3.2 fusion.23
  443.1 2.4 all-to-all-done.4
  445.5 12.0 all-to-all-start.1
  461.8 3.0 reshape.440
  464.8 2.2 copy.382
  467.1 10.0 all-to-all-done.1
  484.4 3.0 collective-permute-start.5
  488.0 2.7 copy.377
  490.7 2.8 reshape.437
  493.5 4.5 all-to-all-start.2
  497.9 62.6 %all_gather.27 = f32[8,4,2,360]{3,1,2,0:T(4,128)S(1)} all-gather(f32[1,4,2,360]{3,1,2,0:T(4,128)S(1)} %copy.318), channel_id=1, replica_groups=mesh['lev'=4,'tile'=64,'sec'=2] {'lev','sec'}, dimensions={0}, use_global_device_ids=true | all-gather | bytes 103680 | tf_op jit(solution)/shard_map/all_gather | solution.py:30
  563.1 63.3 %all_gather.26 = f32[8,4,2,360]{3,1,2,0:T(4,128)S(1)} all-gather(f32[1,4,2,360]{3,1,2,0:T(4,128)S(1)} %copy.317), channel_id=1, replica_groups=mesh['lev'=4,'tile'=64,'sec'=2] {'lev','sec'}, dimensions={0}, use_global_device_ids=true | all-gather | bytes 103680 | tf_op jit(solution)/shard_map/all_gather | solution.py:30
  627.4 3.0 reshape.438
  638.0 14.9 all-to-all-start.5
  656.1 10.7 all-to-all-done.5
  666.8 5.6 all-to-all-start.3
  677.4 3.6 collective-permute-start.13
  681.1 2.7 copy.383
  683.8 2.8 reshape.441
  688.7 14.6 all-to-all-start.6
  704.9 62.2 %all_gather.31 = f32[8,4,2,360]{3,1,2,0:T(4,128)S(1)} all-gather(f32[1,4,2,360]{3,1,2,0:T(4,128)S(1)} %copy.357), channel_id=1, replica_groups=mesh['lev'=4,'tile'=64,'sec'=2] {'lev','sec'}, dimensions={0}, use_global_device_ids=true | all-gather | bytes 103680 | tf_op jit(solution)/shard_map/all_gather | solution.py:30
  769.2 63.2 %all_gather.30 = f32[8,4,2,360]{3,1,2,0:T(4,128)S(1)} all-gather(f32[1,4,2,360]{3,1,2,0:T(4,128)S(1)} %copy.356), channel_id=1, replica_groups=mesh['lev'=4,'tile'=64,'sec'=2] {'lev','sec'}, dimensions={0}, use_global_device_ids=true | all-gather | bytes 103680 | tf_op jit(solution)/shard_map/all_gather | solution.py:30
  833.4 160.5 %all-reduce.8.cloned.1.call-done = (f32[4,2,360]{2,1,0:T(2,128)}, f32[4,2,360]{2,1,0:T(2,128)}, f32[4,2,360]{2,1,0:T(2,128)}, f32[4,2,360]{2,1,0:T(2,128)}, f32[4,2,360]{2,1,0:T(2,128)}, /*index=5*/f32[4,2,360]{2,1,0:T(2,128)}) async-done(((f32[4,2,360]{2,1,0:T(2,128)}, f32[4,2,360]{2,1,0:T(2,128)}, f32[4,2,360]{2,1,0:T(2,128)}, f32[4,2,360]{2,1,0:T(2,128)}, f32[4,2,360]{2,1,0:T(2,128)}, ...) | async-done | bytes 69136 | tf_op jit(solution)/shard_map/psum | solution.py:69
  1001.3 3.0 collective-permute-start.15
  1005.6 3.5 collective-permute-start.7
  1012.4 3.0 reshape.442
  1015.4 2.2 copy.385
  1023.6 4.7 all-to-all-start.7
  1029.3 2.1 convolution_add_fusion
  1031.5 112.3 %psum.131 = f32[2,384]{1,0:T(2,128)} all-reduce(f32[2,384]{1,0:T(2,128)S(1)} %maximum_add_fusion.2), channel_id=1, replica_groups=mesh['lev'=4,'tile'=64,'sec'=2] {'lev','tile','sec'}, use_global_device_ids=true, to_apply=%region_32.33 | all-reduce | flops 768 | bytes 6144 | tf_op jit(solution)/shard_map/psum | solution.py:187
  1144.8 368.7 %all-reduce.6.cloned.1.call-done = (f32[192,384]{1,0:T(8,128)}, f32[384,384]{1,0:T(8,128)}, f32[384,192]{0,1:T(8,128)}) async-done(((f32[192,384]{1,0:T(8,128)}, f32[384,384]{1,0:T(8,128)}, f32[384,192]{0,1:T(8,128)}), (f32[192,384]{1,0:T(8,128)}, f32[384,384]{1,0:T(8,128)}, f32[384,192]{0,1:T(8,128)})) %all-reduce.6.cloned.1.call-update) | async-done | bytes 1179664 | tf_op jit(solution)/shard_map/psum | solution.py:187
  (371 shorter events, 105.7 us)
Async XLA Ops:
  8.0 431.8 %copy-start = (bf16[384,384]{1,0:T(8,128)(2,1)S(1)}, bf16[384,384]{1,0:T(8,128)(2,1)}, u32[]{:S(2)}) copy-start(bf16[384,384]{1,0:T(8,128)(2,1)} %param.23) | copy-start | bytes 884740
  10.4 262.7 %collective-permute-start = (f32[8,4,1,360]{3,2,1,0:T(1,128)}, f32[8,4,1,360]{3,2,1,0:T(1,128)}, u32[]{:S(2)}, u32[]{:S(2)}) collective-permute-start(f32[8,4,1,360]{3,2,1,0:T(1,128)} %get-tuple-element.434), channel_id=1, source_target_pairs={{2,0},{4,2},{6,4},{8,6},{10,8},{12,10},{14,12},{16,14},{18,16},{20... | collective-permute-start | bytes 138248 | tf_op jit(solution)/shard_map/ppermute | solution.py:23
  11.7 261.4 %collective-permute-start.1 = (f32[8,4,1,360]{3,2,1,0:T(1,128)}, f32[8,4,1,360]{3,2,1,0:T(1,128)}, u32[]{:S(2)}, u32[]{:S(2)}) collective-permute-start(f32[8,4,1,360]{3,2,1,0:T(1,128)} %get-tuple-element.435), channel_id=1, source_target_pairs={{0,2},{2,4},{4,6},{6,8},{8,10},{10,12},{12,14},{14,16},{16,18},{18... | collective-permute-start | bytes 138248 | tf_op jit(solution)/shard_map/ppermute | solution.py:22
  18.4 323.5 %collective-permute-start.8 = (f32[8,4,1,360]{3,2,1,0:T(1,128)}, f32[8,4,1,360]{3,2,1,0:T(1,128)}, u32[]{:S(2)}, u32[]{:S(2)}) collective-permute-start(f32[8,4,1,360]{3,2,1,0:T(1,128)} %get-tuple-element.408), channel_id=1, source_target_pairs={{2,0},{4,2},{6,4},{8,6},{10,8},{12,10},{14,12},{16,14},{18,16},{20... | collective-permute-start | bytes 138248 | tf_op jit(solution)/shard_map/ppermute | solution.py:23
  19.7 322.2 %collective-permute-start.9 = (f32[8,4,1,360]{3,2,1,0:T(1,128)}, f32[8,4,1,360]{3,2,1,0:T(1,128)}, u32[]{:S(2)}, u32[]{:S(2)}) collective-permute-start(f32[8,4,1,360]{3,2,1,0:T(1,128)} %get-tuple-element.409), channel_id=1, source_target_pairs={{0,2},{2,4},{4,6},{6,8},{8,10},{10,12},{12,14},{14,16},{16,18},{18... | collective-permute-start | bytes 138248 | tf_op jit(solution)/shard_map/ppermute | solution.py:22
  32.7 390.2 %all-to-all-start = ((bf16[8,2,4320]{2,1,0:T(2,128)(2,1)}), bf16[8,2,4320]{2,1,0:T(2,128)(2,1)}, u32[]{:S(2)}, u32[]{:S(2)}) async-start(bf16[8,2,4320]{2,1,0:T(2,128)(2,1)} %reshape.435), calls=%async_computation | async-start | bytes 278528 | tf_op jit(solution)/shard_map/all_to_all | solution.py:97
  60.6 143.6 %copy-start.40 = (f32[8,4,2,360]{3,2,1,0:T(2,128)}, f32[8,4,2,360]{3,2,1,0:T(2,128)S(1)}, u32[]{:S(2)}) copy-start(f32[8,4,2,360]{3,2,1,0:T(2,128)S(1)} %fusion.183) | copy-start | bytes 276484
  209.7 132.2 %copy-start.20 = (f32[8,4,2,360]{3,2,1,0:T(2,128)S(1)}, f32[8,4,2,360]{3,2,1,0:T(2,128)}, u32[]{:S(2)}) copy-start(f32[8,4,2,360]{3,2,1,0:T(2,128)} %copy-done.19) | copy-start | bytes 276484
  209.8 132.2 %copy-start.43 = (f32[8,4,2,359]{3,2,1,0:T(2,128)S(1)}, f32[8,4,2,359]{3,2,1,0:T(2,128)}, u32[]{:S(2)}) copy-start(f32[8,4,2,359]{3,2,1,0:T(2,128)} %get-tuple-element.406) | copy-start | bytes 275716
  209.8 132.2 %copy-start.44 = (f32[8,4,2,359]{3,2,1,0:T(2,128)S(1)}, f32[8,4,2,359]{3,2,1,0:T(2,128)}, u32[]{:S(2)}) copy-start(f32[8,4,2,359]{3,2,1,0:T(2,128)} %get-tuple-element.407) | copy-start | bytes 275716
  209.8 132.2 %copy-start.54 = (f32[8,4,2,1]{3,2,1,0:T(2,128)S(1)}, f32[8,4,2,1]{3,2,1,0:T(2,128)}, u32[]{:S(2)}) copy-start(f32[8,4,2,1]{3,2,1,0:T(2,128)} %get-tuple-element.404) | copy-start | bytes 772
  209.8 132.2 %copy-start.55 = (f32[8,4,2,1]{3,2,1,0:T(2,128)S(1)}, f32[8,4,2,1]{3,2,1,0:T(2,128)}, u32[]{:S(2)}) copy-start(f32[8,4,2,1]{3,2,1,0:T(2,128)} %get-tuple-element.405) | copy-start | bytes 772
  209.8 198.5 %copy-start.65 = (f32[8]{0:T(128)S(1)}, f32[8]{0:T(128)}, u32[]{:S(2)}) copy-start(f32[8]{0:T(128)} %copy-done.64) | copy-start | bytes 100
  209.8 199.2 %copy-start.39 = (f32[8,4,2,360]{3,2,1,0:T(2,128)S(1)}, f32[8,4,2,360]{3,2,1,0:T(2,128)}, u32[]{:S(2)}) copy-start(f32[8,4,2,360]{3,2,1,0:T(2,128)} %copy-done.38) | copy-start | bytes 276484
  209.8 199.2 %copy-start.63 = (f32[4,2,360]{2,1,0:T(2,128)S(1)}, f32[4,2,360]{2,1,0:T(2,128)}, u32[]{:S(2)}) copy-start(f32[4,2,360]{2,1,0:T(2,128)} %get-tuple-element.346) | copy-start | bytes 34564
  209.8 199.2 %copy-start.58 = (f32[4,2,360]{2,1,0:T(2,128)S(1)}, f32[4,2,360]{2,1,0:T(2,128)}, u32[]{:S(2)}) copy-start(f32[4,2,360]{2,1,0:T(2,128)} %param.20) | copy-start | bytes 34564
  273.1 147.9 %copy-start.61 = (f32[2]{0:T(128)S(1)}, f32[2]{0:T(128)}, u32[]{:S(2)}) copy-start(f32[2]{0:T(128)} %fusion.149) | copy-start | bytes 28
  410.4 48.5 %collective-permute-start.2 = (f32[8,4,1,360]{3,2,1,0:T(1,128)}, f32[8,4,1,360]{3,2,1,0:T(1,128)}, u32[]{:S(2)}, u32[]{:S(2)}) collective-permute-start(f32[8,4,1,360]{3,2,1,0:T(1,128)} %get-tuple-element.426), channel_id=1, source_target_pairs={{2,0},{4,2},{6,4},{8,6},{10,8},{12,10},{14,12},{16,14},{18,16},{20... | collective-permute-start | bytes 138248 | tf_op jit(solution)/shard_map/ppermute | solution.py:23
  411.7 47.2 %collective-permute-start.3 = (f32[8,4,1,360]{3,2,1,0:T(1,128)}, f32[8,4,1,360]{3,2,1,0:T(1,128)}, u32[]{:S(2)}, u32[]{:S(2)}) collective-permute-start(f32[8,4,1,360]{3,2,1,0:T(1,128)} %get-tuple-element.427), channel_id=1, source_target_pairs={{0,2},{2,4},{4,6},{6,8},{8,10},{10,12},{12,14},{14,16},{16,18},{18... | collective-permute-start | bytes 138248 | tf_op jit(solution)/shard_map/ppermute | solution.py:22
  415.9 43.0 %collective-permute-start.10 = (f32[8,4,1,360]{3,2,1,0:T(1,128)}, f32[8,4,1,360]{3,2,1,0:T(1,128)}, u32[]{:S(2)}, u32[]{:S(2)}) collective-permute-start(f32[8,4,1,360]{3,2,1,0:T(1,128)} %get-tuple-element.398), channel_id=1, source_target_pairs={{2,0},{4,2},{6,4},{8,6},{10,8},{12,10},{14,12},{16,14},{18,16},{20... | collective-permute-start | bytes 138248 | tf_op jit(solution)/shard_map/ppermute | solution.py:23
  417.2 41.7 %collective-permute-start.11 = (f32[8,4,1,360]{3,2,1,0:T(1,128)}, f32[8,4,1,360]{3,2,1,0:T(1,128)}, u32[]{:S(2)}, u32[]{:S(2)}) collective-permute-start(f32[8,4,1,360]{3,2,1,0:T(1,128)} %get-tuple-element.399), channel_id=1, source_target_pairs={{0,2},{2,4},{4,6},{6,8},{8,10},{10,12},{12,14},{14,16},{16,18},{18... | collective-permute-start | bytes 138248 | tf_op jit(solution)/shard_map/ppermute | solution.py:22
  422.9 22.5 %all-to-all-start.4 = ((bf16[8,2,4320]{2,1,0:T(2,128)(2,1)}), bf16[8,2,4320]{2,1,0:T(2,128)(2,1)}, u32[]{:S(2)}, u32[]{:S(2)}) async-start(bf16[8,2,4320]{2,1,0:T(2,128)(2,1)} %reshape.439), calls=%async_computation.4 | async-start | bytes 278528 | tf_op jit(solution)/shard_map/all_to_all | solution.py:97
  445.5 31.6 %all-to-all-start.1 = ((bf16[3,64,360]{2,0,1:T(4,128)(2,1)}), bf16[3,64,360]{2,0,1:T(4,128)(2,1)}, u32[]{:S(2)}, u32[]{:S(2)}) async-start(bf16[3,64,360]{2,0,1:T(4,128)(2,1)} %copy.308), calls=%async_computation.1 | async-start | bytes 393216 | tf_op jit(solution)/shard_map/all_to_all | solution.py:102
  483.1 77.5 %collective-permute-start.4 = (f32[8,4,1,360]{3,2,1,0:T(1,128)}, f32[8,4,1,360]{3,2,1,0:T(1,128)S(1)}, u32[]{:S(2)}, u32[]{:S(2)}) collective-permute-start(f32[8,4,1,360]{3,2,1,0:T(1,128)} %get-tuple-element.420), channel_id=1, source_target_pairs={{2,0},{4,2},{6,4},{8,6},{10,8},{12,10},{14,12},{16,14},{18,16},{20... | collective-permute-start | bytes 138248 | tf_op jit(solution)/shard_map/ppermute | solution.py:23
  484.4 76.2 %collective-permute-start.5 = (f32[8,4,1,360]{3,2,1,0:T(1,128)}, f32[8,4,1,360]{3,2,1,0:T(1,128)S(1)}, u32[]{:S(2)}, u32[]{:S(2)}) collective-permute-start(f32[8,4,1,360]{3,2,1,0:T(1,128)} %get-tuple-element.421), channel_id=1, source_target_pairs={{0,2},{2,4},{4,6},{6,8},{8,10},{10,12},{12,14},{14,16},{16,18},{18... | collective-permute-start | bytes 138248 | tf_op jit(solution)/shard_map/ppermute | solution.py:22
  493.5 133.9 %all-to-all-start.2 = ((bf16[8,2,4320]{2,1,0:T(2,128)(2,1)}), bf16[8,2,4320]{2,1,0:T(2,128)(2,1)}, u32[]{:S(2)}, u32[]{:S(2)}) async-start(bf16[8,2,4320]{2,1,0:T(2,128)(2,1)} %reshape.437), calls=%async_computation.2 | async-start | bytes 278528 | tf_op jit(solution)/shard_map/all_to_all | solution.py:97
  638.0 28.9 %all-to-all-start.5 = ((bf16[3,64,360]{2,0,1:T(4,128)(2,1)}), bf16[3,64,360]{2,0,1:T(4,128)(2,1)S(1)}, u32[]{:S(2)}, u32[]{:S(2)}) async-start(bf16[3,64,360]{2,0,1:T(4,128)(2,1)} %copy.349), calls=%async_computation.5 | async-start | bytes 393216 | tf_op jit(solution)/shard_map/all_to_all | solution.py:102
  666.8 21.9 %all-to-all-start.3 = ((bf16[3,64,360]{2,0,1:T(4,128)(2,1)}), bf16[3,64,360]{2,0,1:T(4,128)(2,1)}, u32[]{:S(2)}, u32[]{:S(2)}) async-start(bf16[3,64,360]{2,0,1:T(4,128)(2,1)} %copy.333), calls=%async_computation.3 | async-start | bytes 393216 | tf_op jit(solution)/shard_map/all_to_all | solution.py:102
  676.2 91.0 %collective-permute-start.12 = (f32[8,4,1,360]{3,2,1,0:T(1,128)}, f32[8,4,1,360]{3,2,1,0:T(1,128)}, u32[]{:S(2)}, u32[]{:S(2)}) collective-permute-start(f32[8,4,1,360]{3,2,1,0:T(1,128)} %get-tuple-element.392), channel_id=1, source_target_pairs={{2,0},{4,2},{6,4},{8,6},{10,8},{12,10},{14,12},{16,14},{18,16},{20... | collective-permute-start | bytes 138248 | tf_op jit(solution)/shard_map/ppermute | solution.py:23
  677.4 89.7 %collective-permute-start.13 = (f32[8,4,1,360]{3,2,1,0:T(1,128)}, f32[8,4,1,360]{3,2,1,0:T(1,128)}, u32[]{:S(2)}, u32[]{:S(2)}) collective-permute-start(f32[8,4,1,360]{3,2,1,0:T(1,128)} %get-tuple-element.393), channel_id=1, source_target_pairs={{0,2},{2,4},{4,6},{6,8},{8,10},{10,12},{12,14},{14,16},{16,18},{18... | collective-permute-start | bytes 138248 | tf_op jit(solution)/shard_map/ppermute | solution.py:22
  686.6 146.1 %copy-start.67 = (f32[8]{0:T(128)S(1)}, f32[8]{0:T(128)}, u32[]{:S(2)}) copy-start(f32[8]{0:T(128)} %copy-done.64) | copy-start | bytes 100
  686.6 307.4 %copy-start.59 = (f32[4,2,360]{2,1,0:T(2,128)S(1)}, f32[4,2,360]{2,1,0:T(2,128)}, u32[]{:S(2)}) copy-start(f32[4,2,360]{2,1,0:T(2,128)} %param.20) | copy-start | bytes 34564
  686.6 309.7 %copy-start.37 = (f32[8,4,2,360]{3,2,1,0:T(2,128)S(1)}, f32[8,4,2,360]{3,2,1,0:T(2,128)}, u32[]{:S(2)}) copy-start(f32[8,4,2,360]{3,2,1,0:T(2,128)} %copy-done.36) | copy-start | bytes 276484
  686.6 310.4 %copy-start.60 = (f32[4,2,360]{2,1,0:T(2,128)S(1)}, f32[4,2,360]{2,1,0:T(2,128)}, u32[]{:S(2)}) copy-start(f32[4,2,360]{2,1,0:T(2,128)} %param.18) | copy-start | bytes 34564
  688.7 320.5 %copy-start.18 = (f32[1,8,4,2,360]{4,1,3,2,0:T(8,128)S(1)}, f32[1,8,4,2,360]{4,1,3,2,0:T(8,128)}, u32[]{:S(2)}) copy-start(f32[1,8,4,2,360]{4,1,3,2,0:T(8,128)} %copy-done.17) | copy-start | bytes 276484
  688.7 320.5 %copy-start.62 = (f32[2]{0:T(128)S(1)}, f32[2]{0:T(128)}, u32[]{:S(2)}) copy-start(f32[2]{0:T(128)} %fusion.149) | copy-start | bytes 28
  688.7 323.7 %all-to-all-start.6 = ((bf16[8,2,4320]{2,1,0:T(2,128)(2,1)}), bf16[8,2,4320]{2,1,0:T(2,128)(2,1)}, u32[]{:S(2)}, u32[]{:S(2)}) async-start(bf16[8,2,4320]{2,1,0:T(2,128)(2,1)} %reshape.441), calls=%async_computation.6 | async-start | bytes 278528 | tf_op jit(solution)/shard_map/all_to_all | solution.py:97
  703.3 290.7 %all-reduce.8.cloned.1.call-start = ((), (), s32[]{:S(2)}) async-start(), calls=%async_computation.9 | async-start | bytes 147456 | tf_op jit(solution)/shard_map/psum | solution.py:69
  704.2 305.3 %copy-start.4 = (f32[3,8,4,2,360]{4,1,3,2,0:T(8,128)S(1)}, f32[3,8,4,2,360]{4,1,3,2,0:T(8,128)}, u32[]{:S(2)}) copy-start(f32[3,8,4,2,360]{4,1,3,2,0:T(8,128)} %copy-done.3) | copy-start | bytes 829444
  767.1 243.2 %copy-start.24 = (f32[1,8,4,2,360]{4,1,3,2,0:T(8,128)S(1)}, f32[1,8,4,2,360]{4,1,3,2,0:T(8,128)}, u32[]{:S(2)}) copy-start(f32[1,8,4,2,360]{4,1,3,2,0:T(8,128)} %copy-done.23) | copy-start | bytes 276484
  767.1 243.2 %copy-start.26 = (f32[1,8,4,2,360]{4,1,3,2,0:T(8,128)S(1)}, f32[1,8,4,2,360]{4,1,3,2,0:T(8,128)}, u32[]{:S(2)}) copy-start(f32[1,8,4,2,360]{4,1,3,2,0:T(8,128)} %copy-done.25) | copy-start | bytes 276484
  832.5 179.0 %copy-start.41 = (f32[1,8,4,2,360]{4,1,3,2,0:T(8,128)S(1)}, f32[1,8,4,2,360]{4,1,3,2,0:T(8,128)}, u32[]{:S(2)}) copy-start(f32[1,8,4,2,360]{4,1,3,2,0:T(8,128)} %fusion.131) | copy-start | bytes 276484
  1000.0 10.3 collective-permute-start.14
  1001.3 9.0 collective-permute-start.15
  1004.3 6.0 collective-permute-start.6
  1005.6 4.7 collective-permute-start.7
  1023.6 120.2 %all-to-all-start.7 = ((bf16[3,64,360]{2,0,1:T(4,128)(2,1)}), bf16[3,64,360]{2,0,1:T(4,128)(2,1)S(1)}, u32[]{:S(2)}, u32[]{:S(2)}) async-start(bf16[3,64,360]{2,0,1:T(4,128)(2,1)} %copy.371), calls=%async_computation.7 | async-start | bytes 393216 | tf_op jit(solution)/shard_map/all_to_all | solution.py:102
  1028.3 485.1 %all-reduce.6.cloned.1.call-start = ((), (), s32[]{:S(2)}) async-start(), calls=%async_computation.8 | async-start | bytes 2359296 | tf_op jit(solution)/shard_map/psum | solution.py:187
  (51 other events, 772.1 us)
Sparse Core Ops, SparseCore 0:
  832.8 161.0 all-reduce.7
Sparse Core Ops, SparseCore 1:
  1036.0 477.4 all-reduce.5
where the time goes:
time: 1530 us
  blocking collectives  694 us (45%)
  waiting for transfers between devices  552 us (36%)
  starting transfers between devices  121 us (8%)
  local copies, waits for them, and re-layouts  89.9 us (6%)
  other arithmetic  30.7 us (2%)
  matrix products  20.7 us (1%)
  between operations  16.9 us (1%)
    all_gather x8, blocking collectives, carried_in(): gathered = jax.tree.map(lambda a: lax.all_gather(a, axis), part)  504 us
    psum x1, waiting for transfers between devices, on_device(): lax.psum((local_grads[0], local_grads[1], local_grads[2], local_grads[3])...  369 us
    psum x1, waiting for transfers between devices, vertical_sums(): lax.psum((rising_part, falling_part), ('lev', 'sec'))  161 us
    psum x1, blocking collectives, on_device(): lax.psum((local_grads[0], local_grads[1], local_grads[2], local_grads[3])...  112 us
    psum x1, blocking collectives, vertical_sums(): lax.psum((rising_part, falling_part), ('lev', 'sec'))  78.4 us
    all_to_all x4, starting transfers between devices, to_columns(): lax.all_to_all(flattened, ('lev', 'sec'), split_axis=2, concat_axis=1, ti...  45.6 us
    all_to_all x4, starting transfers between devices, to_levels(): lax.all_to_all(regrouped, ('lev', 'sec'), split_axis=1, concat_axis=2, ti...  37.3 us
    unnamed x164, local copies, waits for them, and re-layouts  35 us
  transfers between devices with their start and end apart: 26, of which 5 were waited for; matrix products, arithmetic and copies ran while one was open for 7% of the time, Pallas kernels for 0%

commit v1 on v0

--- a/solution.py
+++ b/solution.py
@@ -185,7 +185,8 @@
         field_bar = field_bar + TIME_STEP * adj_fields + input_levels
         surface_bar = surface_bar + TIME_STEP * column_sum
         summed = lax.psum(
-            (local_grads[0], local_grads[1], local_grads[2], local_grads[3]), ("lev", "tile", "sec")
+            lax.psum((local_grads[0], local_grads[1], local_grads[2], local_grads[3]), "lev"),
+            ("tile", "sec"),
         )
         gradient = jax.tree.map(jnp.add, gradient, summed)
     return (

time: 1530 us -> 1580 us (1.033)
  the two profiles are of different devices: /device:TPU:8 before, /device:TPU:32 now
where the time goes in v1:
time: 1580 us
  blocking collectives  1070 us (68%)
  waiting for transfers between devices  224 us (14%)
  starting transfers between devices  119 us (8%)
  local copies, waits for them, and re-layouts  91.8 us (6%)
  other arithmetic  31.9 us (2%)
  matrix products  19.7 us (1%)
  between operations  16.9 us (1%)
    all_gather x8, blocking collectives, carried_in(): gathered = jax.tree.map(lambda a: lax.all_gather(a, axis), part)  514 us
    psum x1, blocking collectives, on_device(): lax.psum(lax.psum((local_grads[0], local_grads[1], local_grads[2], local_...  471 us
    psum x1, waiting for transfers between devices, vertical_sums(): lax.psum((rising_part, falling_part), ('lev', 'sec'))  146 us
    psum x1, blocking collectives, vertical_sums(): lax.psum((rising_part, falling_part), ('lev', 'sec'))  78.4 us
    psum x1, waiting for transfers between devices, on_device(): lax.psum((local_grads[0], local_grads[1], local_grads[2], local_grads[3])...  47.9 us
    all_to_all x4, starting transfers between devices, to_columns(): lax.all_to_all(flattened, ('lev', 'sec'), split_axis=2, concat_axis=1, ti...  45.2 us
    unnamed x168, local copies, waits for them, and re-layouts  35.7 us
  transfers between devices with their start and end apart: 27, of which 6 were waited for; matrix products, arithmetic and copies ran while one was open for 7% of the time, Pallas kernels for 0%

profile of v1, /device:TPU:32, one launch (start us, length us, event | category | flops | bytes accessed | tf_op | source)
XLA Modules:
  0.0 1575.6 jit_solution(6588474882337429837)
XLA Ops:
  10.4 3.6 collective-permute-start
  19.1 5.7 collective-permute-start.8
  28.5 4.8 copy.305
  33.3 2.8 reshape.435
  36.1 17.7 %all-to-all-start = ((bf16[8,2,4320]{2,1,0:T(2,128)(2,1)}), bf16[8,2,4320]{2,1,0:T(2,128)(2,1)}, u32[]{:S(2)}, u32[]{:S(2)}) async-start(bf16[8,2,4320]{2,1,0:T(2,128)(2,1)} %reshape.435), calls=%async_computation | async-start | bytes 278528 | tf_op jit(solution)/shard_map/all_to_all | solution.py:97
  65.3 65.6 %all_gather.29 = f32[8,4,2,360]{3,1,2,0:T(4,128)} all-gather(f32[1,4,2,360]{3,1,2,0:T(4,128)S(1)} %copy.336), channel_id=1, replica_groups=mesh['lev'=4,'tile'=64,'sec'=2] {'lev','sec'}, dimensions={0}, use_global_device_ids=true | all-gather | bytes 103680 | tf_op jit(solution)/shard_map/all_gather | solution.py:30
  131.5 78.4 %all-reduce.2 = (f32[4,2,360]{2,1,0:T(2,128)}, f32[4,2,360]{2,1,0:T(2,128)}) all-reduce(f32[4,2,360]{2,1,0:T(2,128)S(1)} %get-tuple-element.431, f32[4,2,360]{2,1,0:T(2,128)S(1)} %get-tuple-element.456), channel_id=1, replica_groups=mesh['lev'=4,'tile'=64,'sec'=2] {'lev','sec'}, use_global_device_ids=true, to_apply=%region_1.2 | all-reduce | flops 5760 | bytes 46080 | tf_op jit(solution)/shard_map/psum | solution.py:69
  209.9 2.7 copy.380
  212.7 2.8 reshape.439
  215.5 63.4 %all_gather.25 = f32[8,4,2,360]{3,1,2,0:T(4,128)S(1)} all-gather(f32[1,4,2,360]{3,1,2,0:T(4,128)S(1)} %copy.295), channel_id=1, replica_groups=mesh['lev'=4,'tile'=64,'sec'=2] {'lev','sec'}, dimensions={0}, use_global_device_ids=true | all-gather | bytes 103680 | tf_op jit(solution)/shard_map/all_gather | solution.py:30
  281.0 63.1 %all_gather.24 = f32[8,4,2,360]{3,1,2,0:T(4,128)S(1)} all-gather(f32[1,4,2,360]{3,1,2,0:T(4,128)S(1)} %copy.294), channel_id=1, replica_groups=mesh['lev'=4,'tile'=64,'sec'=2] {'lev','sec'}, dimensions={0}, use_global_device_ids=true | all-gather | bytes 103680 | tf_op jit(solution)/shard_map/all_gather | solution.py:30
  349.3 63.1 %all_gather.28 = f32[8,4,2,360]{3,1,2,0:T(4,128)S(1)} all-gather(f32[1,4,2,360]{3,1,2,0:T(4,128)S(1)} %copy.335), channel_id=1, replica_groups=mesh['lev'=4,'tile'=64,'sec'=2] {'lev','sec'}, dimensions={0}, use_global_device_ids=true | all-gather | bytes 103680 | tf_op jit(solution)/shard_map/all_gather | solution.py:30
  416.6 2.4 collective-permute-start.3
  419.5 5.3 collective-permute-start.10
  428.8 7.3 all-to-all-start.4
  436.1 3.0 reshape.436
  439.1 2.2 copy.376
  441.3 3.2 fusion.23
  447.8 6.4 all-to-all-done.4
  454.3 8.0 all-to-all-start.1
  466.6 3.0 reshape.440
  469.6 2.2 copy.382
  471.8 10.2 all-to-all-done.1
  489.9 2.4 collective-permute-start.5
  492.9 2.7 copy.377
  495.7 2.8 reshape.437
  498.4 6.5 all-to-all-start.2
  504.9 65.5 %all_gather.27 = f32[8,4,2,360]{3,1,2,0:T(4,128)S(1)} all-gather(f32[1,4,2,360]{3,1,2,0:T(4,128)S(1)} %copy.318), channel_id=1, replica_groups=mesh['lev'=4,'tile'=64,'sec'=2] {'lev','sec'}, dimensions={0}, use_global_device_ids=true | all-gather | bytes 103680 | tf_op jit(solution)/shard_map/all_gather | solution.py:30
  572.9 63.4 %all_gather.26 = f32[8,4,2,360]{3,1,2,0:T(4,128)S(1)} all-gather(f32[1,4,2,360]{3,1,2,0:T(4,128)S(1)} %copy.317), channel_id=1, replica_groups=mesh['lev'=4,'tile'=64,'sec'=2] {'lev','sec'}, dimensions={0}, use_global_device_ids=true | all-gather | bytes 103680 | tf_op jit(solution)/shard_map/all_gather | solution.py:30
  637.0 3.0 reshape.438
  647.6 12.1 all-to-all-start.5
  663.0 12.4 all-to-all-done.5
  675.4 4.0 all-to-all-start.3
  685.7 2.4 collective-permute-start.13
  688.1 2.7 copy.383
  690.9 2.7 reshape.441
  695.3 13.8 all-to-all-start.6
  711.4 66.4 %all_gather.31 = f32[8,4,2,360]{3,1,2,0:T(4,128)S(1)} all-gather(f32[1,4,2,360]{3,1,2,0:T(4,128)S(1)} %copy.357), channel_id=1, replica_groups=mesh['lev'=4,'tile'=64,'sec'=2] {'lev','sec'}, dimensions={0}, use_global_device_ids=true | all-gather | bytes 103680 | tf_op jit(solution)/shard_map/all_gather | solution.py:30
  779.7 63.1 %all_gather.30 = f32[8,4,2,360]{3,1,2,0:T(4,128)S(1)} all-gather(f32[1,4,2,360]{3,1,2,0:T(4,128)S(1)} %copy.356), channel_id=1, replica_groups=mesh['lev'=4,'tile'=64,'sec'=2] {'lev','sec'}, dimensions={0}, use_global_device_ids=true | all-gather | bytes 103680 | tf_op jit(solution)/shard_map/all_gather | solution.py:30
  843.6 146.3 %all-reduce.10.cloned.1.call-done = (f32[4,2,360]{2,1,0:T(2,128)}, f32[4,2,360]{2,1,0:T(2,128)}, f32[4,2,360]{2,1,0:T(2,128)}, f32[4,2,360]{2,1,0:T(2,128)}, f32[4,2,360]{2,1,0:T(2,128)}, /*index=5*/f32[4,2,360]{2,1,0:T(2,128)}) async-done(((f32[4,2,360]{2,1,0:T(2,128)}, f32[4,2,360]{2,1,0:T(2,128)}, f32[4,2,360]{2,1,0:T(2,128)}, f32[4,2,360]{2,1,0:T(2,128)}, f32[4,2,360]{2,1,0:T(2,128)}, ...) | async-done | bytes 69136 | tf_op jit(solution)/shard_map/psum | solution.py:69
  999.2 2.4 collective-permute-start.14
  1003.6 5.9 collective-permute-start.6
  1013.1 3.0 reshape.442
  1016.0 2.2 copy.385
  1027.0 3.8 all-to-all-start.7
  1033.2 47.9 %all-reduce.12.cloned.1.call-done = (f32[192,384]{1,0:T(8,128)}, f32[384,384]{1,0:T(8,128)}, f32[384,192]{0,1:T(8,128)}) async-done(((f32[192,384]{1,0:T(8,128)}, f32[384,384]{1,0:T(8,128)}, f32[384,192]{0,1:T(8,128)}), (f32[192,384]{1,0:T(8,128)}, f32[384,384]{1,0:T(8,128)}, f32[384,192]{0,1:T(8,128)})) %all-reduce.12.cloned.1.call-update) | async-done | bytes 1179664 | tf_op jit(solution)/shard_map/psum | solution.py:188
  1081.2 9.3 psum.199
  1090.5 471.4 %psum.195 = f32[2,384]{1,0:T(2,128)} all-reduce(f32[2,384]{1,0:T(2,128)S(1)} %psum.199), channel_id=1, replica_groups=mesh['lev'=4,'tile'=64,'sec'=2] {'tile','sec'}, use_global_device_ids=true, to_apply=%region_39.40 | all-reduce | flops 768 | bytes 6144 | tf_op jit(solution)/shard_map/psum | solution.py:187
  (355 shorter events, 113.7 us)
Async XLA Ops:
  8.0 436.5 %copy-start = (bf16[384,384]{1,0:T(8,128)(2,1)S(1)}, bf16[384,384]{1,0:T(8,128)(2,1)}, u32[]{:S(2)}) copy-start(bf16[384,384]{1,0:T(8,128)(2,1)} %param.23) | copy-start | bytes 884740
  10.4 268.5 %collective-permute-start = (f32[8,4,1,360]{3,2,1,0:T(1,128)}, f32[8,4,1,360]{3,2,1,0:T(1,128)}, u32[]{:S(2)}, u32[]{:S(2)}) collective-permute-start(f32[8,4,1,360]{3,2,1,0:T(1,128)} %get-tuple-element.437), channel_id=1, source_target_pairs={{2,0},{4,2},{6,4},{8,6},{10,8},{12,10},{14,12},{16,14},{18,16},{20... | collective-permute-start | bytes 138248 | tf_op jit(solution)/shard_map/ppermute | solution.py:23
  14.1 264.8 %collective-permute-start.1 = (f32[8,4,1,360]{3,2,1,0:T(1,128)}, f32[8,4,1,360]{3,2,1,0:T(1,128)}, u32[]{:S(2)}, u32[]{:S(2)}) collective-permute-start(f32[8,4,1,360]{3,2,1,0:T(1,128)} %get-tuple-element.438), channel_id=1, source_target_pairs={{0,2},{2,4},{4,6},{6,8},{8,10},{10,12},{12,14},{14,16},{16,18},{18... | collective-permute-start | bytes 138248 | tf_op jit(solution)/shard_map/ppermute | solution.py:22
  19.1 328.3 %collective-permute-start.8 = (f32[8,4,1,360]{3,2,1,0:T(1,128)}, f32[8,4,1,360]{3,2,1,0:T(1,128)}, u32[]{:S(2)}, u32[]{:S(2)}) collective-permute-start(f32[8,4,1,360]{3,2,1,0:T(1,128)} %get-tuple-element.411), channel_id=1, source_target_pairs={{2,0},{4,2},{6,4},{8,6},{10,8},{12,10},{14,12},{16,14},{18,16},{20... | collective-permute-start | bytes 138248 | tf_op jit(solution)/shard_map/ppermute | solution.py:23
  24.8 322.6 %collective-permute-start.9 = (f32[8,4,1,360]{3,2,1,0:T(1,128)}, f32[8,4,1,360]{3,2,1,0:T(1,128)}, u32[]{:S(2)}, u32[]{:S(2)}) collective-permute-start(f32[8,4,1,360]{3,2,1,0:T(1,128)} %get-tuple-element.412), channel_id=1, source_target_pairs={{0,2},{2,4},{4,6},{6,8},{8,10},{10,12},{12,14},{14,16},{16,18},{18... | collective-permute-start | bytes 138248 | tf_op jit(solution)/shard_map/ppermute | solution.py:22
  33.3 28.5 %copy-start.69 = (f32[2,384]{1,0:T(2,128)S(1)}, f32[2,384]{1,0:T(2,128)}, u32[]{:S(2)}) copy-start(f32[2,384]{1,0:T(2,128)} %param.25) | copy-start | bytes 9220
  33.3 29.1 %copy-start.70 = (s32[2,360]{1,0:T(2,128)S(1)}, s32[2,360]{1,0:T(2,128)}, u32[]{:S(2)}) copy-start(s32[2,360]{1,0:T(2,128)} %param.21) | copy-start | bytes 8644
  36.1 392.7 %all-to-all-start = ((bf16[8,2,4320]{2,1,0:T(2,128)(2,1)}), bf16[8,2,4320]{2,1,0:T(2,128)(2,1)}, u32[]{:S(2)}, u32[]{:S(2)}) async-start(bf16[8,2,4320]{2,1,0:T(2,128)(2,1)} %reshape.435), calls=%async_computation | async-start | bytes 278528 | tf_op jit(solution)/shard_map/all_to_all | solution.py:97
  63.6 146.3 %copy-start.36 = (f32[8,4,2,360]{3,2,1,0:T(2,128)}, f32[8,4,2,360]{3,2,1,0:T(2,128)S(1)}, u32[]{:S(2)}) copy-start(f32[8,4,2,360]{3,2,1,0:T(2,128)S(1)} %fusion.183) | copy-start | bytes 276484
  215.4 132.0 %copy-start.18 = (f32[8,4,2,360]{3,2,1,0:T(2,128)S(1)}, f32[8,4,2,360]{3,2,1,0:T(2,128)}, u32[]{:S(2)}) copy-start(f32[8,4,2,360]{3,2,1,0:T(2,128)} %copy-done.17) | copy-start | bytes 276484
  215.4 132.0 %copy-start.39 = (f32[8,4,2,359]{3,2,1,0:T(2,128)S(1)}, f32[8,4,2,359]{3,2,1,0:T(2,128)}, u32[]{:S(2)}) copy-start(f32[8,4,2,359]{3,2,1,0:T(2,128)} %get-tuple-element.409) | copy-start | bytes 275716
  215.4 132.0 %copy-start.40 = (f32[8,4,2,359]{3,2,1,0:T(2,128)S(1)}, f32[8,4,2,359]{3,2,1,0:T(2,128)}, u32[]{:S(2)}) copy-start(f32[8,4,2,359]{3,2,1,0:T(2,128)} %get-tuple-element.410) | copy-start | bytes 275716
  215.4 132.0 %copy-start.55 = (f32[8,4,2,1]{3,2,1,0:T(2,128)S(1)}, f32[8,4,2,1]{3,2,1,0:T(2,128)}, u32[]{:S(2)}) copy-start(f32[8,4,2,1]{3,2,1,0:T(2,128)} %get-tuple-element.407) | copy-start | bytes 772
  215.4 132.0 %copy-start.56 = (f32[8,4,2,1]{3,2,1,0:T(2,128)S(1)}, f32[8,4,2,1]{3,2,1,0:T(2,128)}, u32[]{:S(2)}) copy-start(f32[8,4,2,1]{3,2,1,0:T(2,128)} %get-tuple-element.408) | copy-start | bytes 772
  215.4 197.0 %copy-start.66 = (f32[8]{0:T(128)S(1)}, f32[8]{0:T(128)}, u32[]{:S(2)}) copy-start(f32[8]{0:T(128)} %copy-done.65) | copy-start | bytes 100
  215.5 197.7 %copy-start.35 = (f32[8,4,2,360]{3,2,1,0:T(2,128)S(1)}, f32[8,4,2,360]{3,2,1,0:T(2,128)}, u32[]{:S(2)}) copy-start(f32[8,4,2,360]{3,2,1,0:T(2,128)} %copy-done.34) | copy-start | bytes 276484
  215.5 197.7 %copy-start.64 = (f32[4,2,360]{2,1,0:T(2,128)S(1)}, f32[4,2,360]{2,1,0:T(2,128)}, u32[]{:S(2)}) copy-start(f32[4,2,360]{2,1,0:T(2,128)} %get-tuple-element.346) | copy-start | bytes 34564
  215.5 197.7 %copy-start.60 = (f32[4,2,360]{2,1,0:T(2,128)S(1)}, f32[4,2,360]{2,1,0:T(2,128)}, u32[]{:S(2)}) copy-start(f32[4,2,360]{2,1,0:T(2,128)} %param.20) | copy-start | bytes 34564
  278.9 148.0 %copy-start.62 = (f32[2]{0:T(128)S(1)}, f32[2]{0:T(128)}, u32[]{:S(2)}) copy-start(f32[2]{0:T(128)} %fusion.149) | copy-start | bytes 28
  414.6 48.9 %collective-permute-start.2 = (f32[8,4,1,360]{3,2,1,0:T(1,128)}, f32[8,4,1,360]{3,2,1,0:T(1,128)}, u32[]{:S(2)}, u32[]{:S(2)}) collective-permute-start(f32[8,4,1,360]{3,2,1,0:T(1,128)} %get-tuple-element.429), channel_id=1, source_target_pairs={{2,0},{4,2},{6,4},{8,6},{10,8},{12,10},{14,12},{16,14},{18,16},{20... | collective-permute-start | bytes 138248 | tf_op jit(solution)/shard_map/ppermute | solution.py:23
  416.6 47.0 %collective-permute-start.3 = (f32[8,4,1,360]{3,2,1,0:T(1,128)}, f32[8,4,1,360]{3,2,1,0:T(1,128)}, u32[]{:S(2)}, u32[]{:S(2)}) collective-permute-start(f32[8,4,1,360]{3,2,1,0:T(1,128)} %get-tuple-element.430), channel_id=1, source_target_pairs={{0,2},{2,4},{4,6},{6,8},{8,10},{10,12},{12,14},{14,16},{16,18},{18... | collective-permute-start | bytes 138248 | tf_op jit(solution)/shard_map/ppermute | solution.py:22
  419.5 44.1 %collective-permute-start.10 = (f32[8,4,1,360]{3,2,1,0:T(1,128)}, f32[8,4,1,360]{3,2,1,0:T(1,128)}, u32[]{:S(2)}, u32[]{:S(2)}) collective-permute-start(f32[8,4,1,360]{3,2,1,0:T(1,128)} %get-tuple-element.401), channel_id=1, source_target_pairs={{2,0},{4,2},{6,4},{8,6},{10,8},{12,10},{14,12},{16,14},{18,16},{20... | collective-permute-start | bytes 138248 | tf_op jit(solution)/shard_map/ppermute | solution.py:23
  424.8 38.8 %collective-permute-start.11 = (f32[8,4,1,360]{3,2,1,0:T(1,128)}, f32[8,4,1,360]{3,2,1,0:T(1,128)}, u32[]{:S(2)}, u32[]{:S(2)}) collective-permute-start(f32[8,4,1,360]{3,2,1,0:T(1,128)} %get-tuple-element.402), channel_id=1, source_target_pairs={{0,2},{2,4},{4,6},{6,8},{8,10},{10,12},{12,14},{14,16},{16,18},{18... | collective-permute-start | bytes 138248 | tf_op jit(solution)/shard_map/ppermute | solution.py:22
  428.8 25.4 %all-to-all-start.4 = ((bf16[8,2,4320]{2,1,0:T(2,128)(2,1)}), bf16[8,2,4320]{2,1,0:T(2,128)(2,1)}, u32[]{:S(2)}, u32[]{:S(2)}) async-start(bf16[8,2,4320]{2,1,0:T(2,128)(2,1)} %reshape.439), calls=%async_computation.4 | async-start | bytes 278528 | tf_op jit(solution)/shard_map/all_to_all | solution.py:97
  454.3 27.7 %all-to-all-start.1 = ((bf16[3,64,360]{2,0,1:T(4,128)(2,1)}), bf16[3,64,360]{2,0,1:T(4,128)(2,1)}, u32[]{:S(2)}, u32[]{:S(2)}) async-start(bf16[3,64,360]{2,0,1:T(4,128)(2,1)} %copy.308), calls=%async_computation.1 | async-start | bytes 393216 | tf_op jit(solution)/shard_map/all_to_all | solution.py:102
  488.0 82.3 %collective-permute-start.4 = (f32[8,4,1,360]{3,2,1,0:T(1,128)}, f32[8,4,1,360]{3,2,1,0:T(1,128)S(1)}, u32[]{:S(2)}, u32[]{:S(2)}) collective-permute-start(f32[8,4,1,360]{3,2,1,0:T(1,128)} %get-tuple-element.423), channel_id=1, source_target_pairs={{2,0},{4,2},{6,4},{8,6},{10,8},{12,10},{14,12},{16,14},{18,16},{20... | collective-permute-start | bytes 138248 | tf_op jit(solution)/shard_map/ppermute | solution.py:23
  489.9 80.4 %collective-permute-start.5 = (f32[8,4,1,360]{3,2,1,0:T(1,128)}, f32[8,4,1,360]{3,2,1,0:T(1,128)S(1)}, u32[]{:S(2)}, u32[]{:S(2)}) collective-permute-start(f32[8,4,1,360]{3,2,1,0:T(1,128)} %get-tuple-element.424), channel_id=1, source_target_pairs={{0,2},{2,4},{4,6},{6,8},{8,10},{10,12},{12,14},{14,16},{16,18},{18... | collective-permute-start | bytes 138248 | tf_op jit(solution)/shard_map/ppermute | solution.py:22
  498.4 138.6 %all-to-all-start.2 = ((bf16[8,2,4320]{2,1,0:T(2,128)(2,1)}), bf16[8,2,4320]{2,1,0:T(2,128)(2,1)}, u32[]{:S(2)}, u32[]{:S(2)}) async-start(bf16[8,2,4320]{2,1,0:T(2,128)(2,1)} %reshape.437), calls=%async_computation.2 | async-start | bytes 278528 | tf_op jit(solution)/shard_map/all_to_all | solution.py:97
  646.5 32.9 %copy-start.12 = (f32[3,8,4,2,360]{4,3,2,1,0:T(2,128)S(1)}, f32[3,8,4,2,360]{4,3,2,1,0:T(2,128)}, u32[]{:S(2)}) copy-start(f32[3,8,4,2,360]{4,3,2,1,0:T(2,128)} %fusion.81) | copy-start | bytes 829444
  647.6 27.8 %all-to-all-start.5 = ((bf16[3,64,360]{2,0,1:T(4,128)(2,1)}), bf16[3,64,360]{2,0,1:T(4,128)(2,1)S(1)}, u32[]{:S(2)}, u32[]{:S(2)}) async-start(bf16[3,64,360]{2,0,1:T(4,128)(2,1)} %copy.349), calls=%async_computation.5 | async-start | bytes 393216 | tf_op jit(solution)/shard_map/all_to_all | solution.py:102
  675.4 19.9 %all-to-all-start.3 = ((bf16[3,64,360]{2,0,1:T(4,128)(2,1)}), bf16[3,64,360]{2,0,1:T(4,128)(2,1)}, u32[]{:S(2)}, u32[]{:S(2)}) async-start(bf16[3,64,360]{2,0,1:T(4,128)(2,1)} %copy.333), calls=%async_computation.3 | async-start | bytes 393216 | tf_op jit(solution)/shard_map/all_to_all | solution.py:102
  683.8 94.0 %collective-permute-start.12 = (f32[8,4,1,360]{3,2,1,0:T(1,128)}, f32[8,4,1,360]{3,2,1,0:T(1,128)}, u32[]{:S(2)}, u32[]{:S(2)}) collective-permute-start(f32[8,4,1,360]{3,2,1,0:T(1,128)} %get-tuple-element.395), channel_id=1, source_target_pairs={{2,0},{4,2},{6,4},{8,6},{10,8},{12,10},{14,12},{16,14},{18,16},{20... | collective-permute-start | bytes 138248 | tf_op jit(solution)/shard_map/ppermute | solution.py:23
  685.7 92.1 %collective-permute-start.13 = (f32[8,4,1,360]{3,2,1,0:T(1,128)}, f32[8,4,1,360]{3,2,1,0:T(1,128)}, u32[]{:S(2)}, u32[]{:S(2)}) collective-permute-start(f32[8,4,1,360]{3,2,1,0:T(1,128)} %get-tuple-element.396), channel_id=1, source_target_pairs={{0,2},{2,4},{4,6},{6,8},{8,10},{10,12},{12,14},{14,16},{16,18},{18... | collective-permute-start | bytes 138248 | tf_op jit(solution)/shard_map/ppermute | solution.py:22
  693.6 149.3 %copy-start.68 = (f32[8]{0:T(128)S(1)}, f32[8]{0:T(128)}, u32[]{:S(2)}) copy-start(f32[8]{0:T(128)} %copy-done.65) | copy-start | bytes 100
  693.6 296.3 %copy-start.33 = (f32[8,4,2,360]{3,2,1,0:T(2,128)S(1)}, f32[8,4,2,360]{3,2,1,0:T(2,128)}, u32[]{:S(2)}) copy-start(f32[8,4,2,360]{3,2,1,0:T(2,128)} %copy-done.32) | copy-start | bytes 276484
  693.6 297.0 %copy-start.59 = (f32[4,2,360]{2,1,0:T(2,128)S(1)}, f32[4,2,360]{2,1,0:T(2,128)}, u32[]{:S(2)}) copy-start(f32[4,2,360]{2,1,0:T(2,128)} %param.18) | copy-start | bytes 34564
  693.6 299.3 %copy-start.61 = (f32[4,2,360]{2,1,0:T(2,128)S(1)}, f32[4,2,360]{2,1,0:T(2,128)}, u32[]{:S(2)}) copy-start(f32[4,2,360]{2,1,0:T(2,128)} %param.20) | copy-start | bytes 34564
  695.3 317.8 %all-to-all-start.6 = ((bf16[8,2,4320]{2,1,0:T(2,128)(2,1)}), bf16[8,2,4320]{2,1,0:T(2,128)(2,1)}, u32[]{:S(2)}, u32[]{:S(2)}) async-start(bf16[8,2,4320]{2,1,0:T(2,128)(2,1)} %reshape.441), calls=%async_computation.6 | async-start | bytes 278528 | tf_op jit(solution)/shard_map/all_to_all | solution.py:97
  709.1 280.8 %all-reduce.10.cloned.1.call-start = ((), (), s32[]{:S(2)}) async-start(), calls=%async_computation.9 | async-start | bytes 147456 | tf_op jit(solution)/shard_map/psum | solution.py:69
  842.9 238.3 %all-reduce.12.cloned.1.call-start = ((), (), s32[]{:S(2)}) async-start(), calls=%async_computation.10 | async-start | bytes 2359296 | tf_op jit(solution)/shard_map/psum | solution.py:188
  999.2 31.6 %collective-permute-start.14 = (f32[8,4,1,360]{3,2,1,0:T(1,128)}, f32[8,4,1,360]{3,2,1,0:T(1,128)}, u32[]{:S(2)}, u32[]{:S(2)}) collective-permute-start(f32[8,4,1,360]{3,2,1,0:T(1,128)} %get-tuple-element.381), channel_id=1, source_target_pairs={{2,0},{4,2},{6,4},{8,6},{10,8},{12,10},{14,12},{16,14},{18,16},{20... | collective-permute-start | bytes 138248 | tf_op jit(solution)/shard_map/ppermute | solution.py:23
  1001.7 29.2 %collective-permute-start.15 = (f32[8,4,1,360]{3,2,1,0:T(1,128)}, f32[8,4,1,360]{3,2,1,0:T(1,128)}, u32[]{:S(2)}, u32[]{:S(2)}) collective-permute-start(f32[8,4,1,360]{3,2,1,0:T(1,128)} %get-tuple-element.382), channel_id=1, source_target_pairs={{0,2},{2,4},{4,6},{6,8},{8,10},{10,12},{12,14},{14,16},{16,18},{18... | collective-permute-start | bytes 138248 | tf_op jit(solution)/shard_map/ppermute | solution.py:22
  1003.6 27.3 %collective-permute-start.6 = (f32[8,4,1,360]{3,2,1,0:T(1,128)}, f32[8,4,1,360]{3,2,1,0:T(1,128)}, u32[]{:S(2)}, u32[]{:S(2)}) collective-permute-start(f32[8,4,1,360]{3,2,1,0:T(1,128)} %get-tuple-element.389), channel_id=1, source_target_pairs={{2,0},{4,2},{6,4},{8,6},{10,8},{12,10},{14,12},{16,14},{18,16},{20... | collective-permute-start | bytes 138248 | tf_op jit(solution)/shard_map/ppermute | solution.py:23
  1009.5 21.4 %collective-permute-start.7 = (f32[8,4,1,360]{3,2,1,0:T(1,128)}, f32[8,4,1,360]{3,2,1,0:T(1,128)}, u32[]{:S(2)}, u32[]{:S(2)}) collective-permute-start(f32[8,4,1,360]{3,2,1,0:T(1,128)} %get-tuple-element.390), channel_id=1, source_target_pairs={{0,2},{2,4},{4,6},{6,8},{8,10},{10,12},{12,14},{14,16},{16,18},{18... | collective-permute-start | bytes 138248 | tf_op jit(solution)/shard_map/ppermute | solution.py:22
  1025.9 536.0 %copy-start.10 = (f32[3,8,4,2,360]{4,1,3,2,0:T(8,128)S(1)}, f32[3,8,4,2,360]{4,1,3,2,0:T(8,128)}, u32[]{:S(2)}) copy-start(f32[3,8,4,2,360]{4,1,3,2,0:T(8,128)} %copy-done.9) | copy-start | bytes 829444
  1025.9 536.0 %copy-start.38 = (f32[1,8,4,2,360]{4,1,3,2,0:T(8,128)S(1)}, f32[1,8,4,2,360]{4,1,3,2,0:T(8,128)}, u32[]{:S(2)}) copy-start(f32[1,8,4,2,360]{4,1,3,2,0:T(8,128)} %fusion.129) | copy-start | bytes 276484
  1027.0 534.9 %all-to-all-start.7 = ((bf16[3,64,360]{2,0,1:T(4,128)(2,1)}), bf16[3,64,360]{2,0,1:T(4,128)(2,1)S(1)}, u32[]{:S(2)}, u32[]{:S(2)}) async-start(bf16[3,64,360]{2,0,1:T(4,128)(2,1)} %copy.371), calls=%async_computation.7 | async-start | bytes 393216 | tf_op jit(solution)/shard_map/all_to_all | solution.py:102
  1030.8 532.1 %all-reduce.8.cloned.1.call-start = ((), (), s32[]{:S(2)}) async-start(), calls=%async_computation.8 | async-start | bytes 2359296 | tf_op jit(solution)/shard_map/psum | solution.py:187
  (54 other events, 336.3 us)
Sparse Core Ops, SparseCore 0:
  843.0 146.8 all-reduce.9
Sparse Core Ops, SparseCore 1:
  1025.4 55.7 all-reduce.11
  1085.2 343.1 all-reduce.7
